TPU v7x, 128 devices: a whole 4x4x4 slice. The times are simulated.
128 devices in a mesh: grp: 16 (over y_lo, z, core), tp: 8 (over x, y_hi).
Axes of the slice: x: 4, y: 4 (y_hi: 2, y_lo: 2; y = y_hi * 2 + y_lo), z: 4, core: 2. Of those that a mesh axis runs over, the one named last changes fastest.
Arguments:
- tokens: bfloat16 [2, 5120, 4096], P(None, 'grp', 'tp'), may hold values from -6 to 6
- norm_gain: float32 [4096], replicated, may hold values from 0.5 to 1.5
- up_master: float32 [4096, 16384], P(('grp', 'tp')), may hold values from -6 to 6
- up_gradient: bfloat16 [4096, 16384], P(('grp', 'tp')), may hold values from -0.59765625 to 0.59765625
- up_first: float32 [4096, 16384], P(('grp', 'tp')), may hold values from -0.18 to 0.18
- up_second: float32 [4096, 16384], P(('grp', 'tp')), may hold values from 0.0001 to 0.01
- down_master: float32 [16384, 4096], P(('grp', 'tp')), may hold values from -6 to 6
- down_gradient: bfloat16 [16384, 4096], P(('grp', 'tp')), may hold values from -0.59765625 to 0.59765625
- down_first: float32 [16384, 4096], P(('grp', 'tp')), may hold values from -0.18 to 0.18
- down_second: float32 [16384, 4096], P(('grp', 'tp')), may hold values from 0.0001 to 0.01
Outputs:
- up_updated: float32 [4096, 16384], P(('grp', 'tp'))
- down_updated: float32 [16384, 4096], P(('grp', 'tp'))
- decoded: bfloat16 [2, 5120, 4096], P(None, 'grp', 'tp')
All inputs are finite; a program needn't handle non-finite values.
Results may differ from a plain program's by a relative error of at most 0.015.
Values may be sent and summed in bfloat16 or wider, within the bound.
No kernel may reach another device: no remote copies, remote signals or barrier semaphores. Data moves between devices by JAX's collectives and lax.ppermute only.
A program may use at most 192 MiB of HBM per device.

v0:
```python
import jax
import jax.numpy as jnp
from jax import lax
from jax.sharding import PartitionSpec as P

learn_rate = 0.05
beta_one = 0.9
beta_two = 0.95
adam_eps = 1e-08
decay_rate = 0.1
step_index = 100
norm_eps = 1e-06


def adamw_update(master, gradient, first_moment, second_moment):
    grad_float = gradient.astype(jnp.float32)
    first_new = beta_one * first_moment + (1.0 - beta_one) * grad_float
    second_new = beta_two * second_moment + (1.0 - beta_two) * grad_float * grad_float
    corr_one = 1.0 - beta_one**step_index
    corr_two = 1.0 - beta_two**step_index
    update = first_new / corr_one / (jnp.sqrt(second_new / corr_two) + adam_eps)
    return master - learn_rate * (update + decay_rate * master)


def body(
    tokens,
    norm_gain,
    up_master,
    up_gradient,
    up_first,
    up_second,
    down_master,
    down_gradient,
    down_first,
    down_second,
):
    up_updated = adamw_update(up_master, up_gradient, up_first, up_second)
    down_updated = adamw_update(down_master, down_gradient, down_first, down_second)
    group_count = lax.axis_size("grp")
    shard_count = lax.axis_size("tp")
    up_rows, hidden_width = up_updated.shape
    block_width = hidden_width // (group_count * shard_count)
    model_width = up_rows * group_count * shard_count
    up_cast = up_updated.astype(jnp.bfloat16).reshape(
        up_rows, group_count, shard_count, block_width
    )
    down_cast = down_updated.astype(jnp.bfloat16)
    owned = lax.all_to_all(up_cast, "tp", split_axis=2, concat_axis=0, tiled=True)
    up_local = lax.all_gather(owned, "grp", axis=0, tiled=True).reshape(
        model_width, group_count * block_width
    )
    features_all = lax.all_gather(tokens, "tp", axis=2, tiled=True)
    step_count, row_count, _ = features_all.shape
    flat_rows = features_all.reshape(step_count * row_count, model_width).astype(jnp.float32)
    mean_sq = jnp.mean(flat_rows * flat_rows, axis=-1, keepdims=True)
    normed = (flat_rows * lax.rsqrt(mean_sq + norm_eps) * norm_gain).astype(jnp.bfloat16)
    hidden = jax.nn.silu(
        jnp.dot(normed, up_local, preferred_element_type=jnp.float32) * model_width ** (-0.5)
    ).astype(jnp.bfloat16)
    down_local = lax.all_gather(down_cast, "grp", axis=0, tiled=True)
    running = jnp.dot(hidden, down_local, preferred_element_type=jnp.float32)
    partial_term = running * hidden_width ** (-0.5)
    summed = lax.psum_scatter(
        partial_term.astype(jnp.bfloat16), "tp", scatter_dimension=1, tiled=True
    )
    decoded = summed.reshape(step_count, row_count, model_width // shard_count)
    return (up_updated, down_updated, decoded)


def solution(mesh):
    in_specs = (
        P(None, "grp", "tp"),
        P(),
        P(("grp", "tp"), None),
        P(("grp", "tp"), None),
        P(("grp", "tp"), None),
        P(("grp", "tp"), None),
        P(("grp", "tp"), None),
        P(("grp", "tp"), None),
        P(("grp", "tp"), None),
        P(("grp", "tp"), None),
    )
    out_specs = (P(("grp", "tp"), None), P(("grp", "tp"), None), P(None, "grp", "tp"))
    return jax.shard_map(body, mesh=mesh, in_specs=in_specs, out_specs=out_specs, check_vma=False)
```

profile of v0, /device:TPU:1, one launch (start us, length us, event | category | flops | bytes accessed | tf_op | source)
XLA Modules:
  0.0 412.3 jit_solution(1639237604253128803)
XLA Ops:
  7.2 0.0 all-gather.4.cloned.1.call-start
  7.2 0.7 all-gather.4.cloned.1.call-update
  7.9 0.0 all-gather.6.cloned.1.call-start
  7.9 6.2 %convert_bitcast_fusion = (bf16[4,8,128,128]{3,1,2,0:T(8,128)(2,1)S(1)}, f32[32,16384]{1,0:T(8,128)}) fusion(f32[32,16384]{1,0:T(8,128)} %param.12, f32[32,16384]{1,0:T(8,128)} %param.15, bf16[32,16384]{1,0:T(8,128)(2,1)} %param.13, f32[32,16384]{1,0:T(8,128)} %param.14), kind=kLoop, calls=%fused_computation.33 | loop fusion | flops 8912896 | bytes 10485760
  14.1 0.2 copy.19
  14.4 0.1 copy.16
  14.5 0.0 copy-start.1
  14.5 0.0 copy-start.2
  14.6 26.2 %all_to_all.18 = bf16[32,16,8,128]{3,1,0,2:T(8,128)(2,1)} all-to-all(bf16[32,16,8,128]{3,1,0,2:T(8,128)(2,1)S(1)} %copy.16), channel_id=1, replica_groups=mesh['grp'=16,'tp'=8] {'tp'}, dimensions={2} | all-to-all | bytes 2097152 | tf_op jit(solution)/shard_map/all_to_all | solution.py:48
  40.8 0.0 all-gather.6.cloned.1.call-update
  40.8 0.0 all-gather.8.cloned.1.call-start
  40.8 0.0 copy-done.1
  40.9 0.0 copy-done.2
  40.9 5.5 %fusion.28 = (bf16[128,4096]{1,0:T(8,128)(2,1)}, f32[128,4096]{1,0:T(8,128)}) fusion(f32[128,4096]{1,0:T(8,128)S(1)} %copy-done.1, f32[128,4096]{1,0:T(8,128)} %param.19, bf16[128,4096]{1,0:T(8,128)(2,1)S(1)} %copy-done.2, f32[128,4096]{1,0:T(8,128)} %param.18), kind=kLoop, calls=%fused_computation.37 | loop fusion | flops 8912896 | bytes 10485760 | tf_op jit(solution)/shard_map/convert_element_type | solution.py:47
  46.4 0.0 copy-start.3
  46.4 0.0 all-gather.8.cloned.1.call-update
  46.4 0.0 reduce-scatter.2.cloned.1.call-start
  46.5 63.5 %all-gather.4.cloned.1.call-done = bf16[2,320,4096]{2,1,0:T(8,128)(2,1)} async-done(((bf16[2,320,512]{2,1,0:T(8,128)(2,1)}), bf16[2,320,4096]{2,1,0:T(8,128)(2,1)}) %all-gather.4.cloned.1.call-update) | async-done | bytes 5242896 | tf_op jit(solution)/shard_map/all_gather | solution.py:52
  109.9 0.0 copy-start
  109.9 3.7 fusion
  113.7 0.0 copy-done.3
  113.7 0.3 copy-done
  114.0 4.5 %fusion.2 = bf16[2,320,4096]{2,1,0:T(8,128)(2,1)} fusion(bf16[2,320,4096]{2,1,0:T(8,128)(2,1)S(1)} %copy-done, f32[4096]{0:T(1024)S(1)} %copy-done.3, f32[2,320]{1,0:T(2,128)S(1)} %add_rsqrt_fusion), kind=kLoop, calls=%fused_computation.4 | loop fusion | flops 10485760 | bytes 10504704 | tf_op jit(solution)/shard_map/convert_element_type | solution.py:56
  118.5 85.0 %all-gather.6.cloned.1.call-done = bf16[4096,16,1,128]{3,1,2,0:T(8,128)(2,1)} async-done(((bf16[256,16,1,128]{3,1,2,0:T(8,128)(2,1)}), bf16[4096,16,1,128]{3,1,2,0:T(8,128)(2,1)}) %all-gather.6.cloned.1.call-update) | async-done | bytes 16777232 | tf_op jit(solution)/shard_map/all_gather | solution.py:49
  203.5 22.2 %copy.18 = bf16[4096,16,1,128]{0,3,1,2:T(8,128)(2,1)} copy(bf16[4096,16,1,128]{3,1,2,0:T(8,128)(2,1)} %all-gather.6.cloned.1.call-done) | data formatting | bytes 33554432 | tf_op jit(solution)/shard_map/all_gather | solution.py:49
  225.7 17.1 %multiply_convert_fusion.1.clone.4 = bf16[640,2048]{1,0:T(8,128)(2,1)S(1)} fusion(bf16[640,4096]{1,0:T(8,128)(2,1)} %bitcast.26, bf16[4096,2048]{0,1:T(8,128)(2,1)} %bitcast.25), kind=kOutput, calls=%fused_computation.6.clone.clone.clone.1 | convolution fusion | flops 10745282560 | bytes 24641536 | tf_op jit(solution)/shard_map/dot_general | solution.py:58
  242.8 55.1 %all-gather.8.cloned.1.call-done = bf16[2048,4096]{1,0:T(8,128)(2,1)} async-done(((bf16[128,4096]{1,0:T(8,128)(2,1)}), bf16[2048,4096]{1,0:T(8,128)(2,1)}) %all-gather.8.cloned.1.call-update) | async-done | bytes 16777232 | tf_op jit(solution)/shard_map/all_gather | solution.py:60
  297.8 16.1 %multiply_convert_fusion = bf16[640,4096]{1,0:T(8,128)(2,1)} fusion(bf16[2048,4096]{1,0:T(8,128)(2,1)} %all-gather.8.cloned.1.call-done, bf16[640,2048]{1,0:T(8,128)(2,1)S(1)} %multiply_convert_fusion.1.clone.4), kind=kOutput, calls=%fused_computation.5 | convolution fusion | flops 10742661120 | bytes 24641536 | tf_op jit(solution)/shard_map/dot_general | solution.py:61
  314.0 0.0 reduce-scatter.2.cloned.1.call-update
  314.0 91.7 %reduce-scatter.2.cloned.1.call-done = bf16[640,512]{1,0:T(8,128)(2,1)} async-done(((bf16[640,4096]{1,0:T(8,128)(2,1)}), bf16[640,512]{1,0:T(8,128)(2,1)}) %reduce-scatter.2.cloned.1.call-update) | async-done | bytes 655376 | tf_op jit(solution)/shard_map/reduce_scatter | solution.py:63
  (1 shorter events, 0.0 us)
Async XLA Ops:
  7.2 102.8 %all-gather.4.cloned.1.call-start = ((), (), s32[]{:S(2)}) async-start(), calls=%async_computation.2 | async-start | bytes 5898240 | tf_op jit(solution)/shard_map/all_gather | solution.py:52
  7.9 195.6 %all-gather.6.cloned.1.call-start = ((), (), s32[]{:S(2)}) async-start(), calls=%async_computation.3 | async-start | bytes 17825792 | tf_op jit(solution)/shard_map/all_gather | solution.py:49
  14.5 26.3 %copy-start.1 = (f32[128,4096]{1,0:T(8,128)S(1)}, f32[128,4096]{1,0:T(8,128)}, u32[]{:S(2)}) copy-start(f32[128,4096]{1,0:T(8,128)} %param.16) | copy-start | bytes 6291460
  14.5 26.3 %copy-start.2 = (bf16[128,4096]{1,0:T(8,128)(2,1)S(1)}, bf16[128,4096]{1,0:T(8,128)(2,1)}, u32[]{:S(2)}) copy-start(bf16[128,4096]{1,0:T(8,128)(2,1)} %param.17) | copy-start | bytes 3145732
  40.8 257.0 %all-gather.8.cloned.1.call-start = ((), (), s32[]{:S(2)}) async-start(), calls=%async_computation.4 | async-start | bytes 17825792 | tf_op jit(solution)/shard_map/all_gather | solution.py:60
  46.4 67.3 %copy-start.3 = (f32[4096]{0:T(1024)S(1)}, f32[4096]{0:T(1024)}, u32[]{:S(2)}) copy-start(f32[4096]{0:T(1024)} %param.11) | copy-start | bytes 49156
  46.4 359.3 %reduce-scatter.2.cloned.1.call-start = ((), (), s32[]{:S(2)}) async-start(), calls=%async_computation.5 | async-start | bytes 5898240 | tf_op jit(solution)/shard_map/reduce_scatter | solution.py:63
  109.9 4.0 copy-start
Sparse Core Ops, SparseCore 0:
  10.2 99.6 all-gather.3
  111.6 91.7 all-gather.5
  205.2 92.6 all-gather.7
  314.1 91.5 reduce-scatter.1
where the time goes:
time: 413 us; the launch traced here: 412 us
  waiting for transfers between devices  296 us (72%)
  matrix products  33.2 us (8%)
  blocking collectives  26.2 us (6%)
  local copies, waits for them, and re-layouts  22.9 us (6%)
  other arithmetic  20 us (5%)
  between operations  13.8 us (3%)
    reduce_scatter x1, waiting for transfers between devices, body(): lax.psum_scatter(partial_term.astype(jnp.bfloat16), 'tp', scatter_dimensi...  91.7 us
    all_gather x1, waiting for transfers between devices, body(): lax.all_gather(owned, 'grp', axis=0, tiled=True)  85 us
    all_gather x1, waiting for transfers between devices, body(): features_all = lax.all_gather(tokens, 'tp', axis=2, tiled=True)  63.5 us
    all_gather x1, waiting for transfers between devices, body(): down_local = lax.all_gather(down_cast, 'grp', axis=0, tiled=True)  55.1 us
    all_to_all x1, blocking collectives, body(): lax.all_to_all(up_cast, 'tp', split_axis=2, concat_axis=0, tiled=True)  26.2 us
    all_gather x1, local copies, waits for them, and re-layouts, body(): lax.all_gather(owned, 'grp', axis=0, tiled=True)  22.2 us
    dot_general x1, matrix products, body(): jnp.dot(normed, up_local, preferred_element_type=jnp.float32)  17.1 us
    dot_general x1, matrix products, body(): running = jnp.dot(hidden, down_local, preferred_element_type=jnp.float32)  16.1 us
  transfers between devices with their start and end apart: 4, of which 4 were waited for; matrix products, arithmetic and copies ran while one was open for 14% of the time, Pallas kernels for 0%

commit v1 on v0

--- a/solution.py
+++ b/solution.py
@@ -49,7 +49,9 @@
     up_local = lax.all_gather(owned, "grp", axis=0, tiled=True).reshape(
         model_width, group_count * block_width
     )
-    features_all = lax.all_gather(tokens, "tp", axis=2, tiled=True)
+    features_all = jnp.concatenate(
+        lax.all_to_all(jnp.stack([tokens] * lax.axis_size("tp")), "tp", 0, 0), axis=2
+    )
     step_count, row_count, _ = features_all.shape
     flat_rows = features_all.reshape(step_count * row_count, model_width).astype(jnp.float32)
     mean_sq = jnp.mean(flat_rows * flat_rows, axis=-1, keepdims=True)

time: 413 us -> 395 us (0.956)
  waiting for transfers between devices: 296 us -> 264 us
  local copies, waits for them, and re-layouts: 22.9 us -> 35.3 us
  starting transfers between devices: 0.16 us -> 5.09 us
    all_to_all x0 -> x1, waiting for transfers between devices: none -> 73.5 us  [body(): lax.all_to_all(jnp.stack([tokens] * lax.axis_size('tp')), 'tp', 0, 0)]
    all_gather x1 -> x0, waiting for transfers between devices: 63.5 us -> none  [body(): features_all = lax.all_gather(tokens, 'tp', axis=2, tiled=True)]
    all_gather x1, waiting for transfers between devices: 85 us -> 43.9 us  [body(): lax.all_gather(owned, 'grp', axis=0, tiled=True)]
    unnamed x9 -> x8, local copies, waits for them, and re-layouts: 0.54 us -> 6.1 us
    all_to_all x0 -> x1, starting transfers between devices: none -> 4.79 us  [body(): lax.all_to_all(jnp.stack([tokens] * lax.axis_size('tp')), 'tp', 0, 0)]
  transfers between devices with their start and end apart: 4 -> 4, of which waited for: 4 -> 4; matrix products, arithmetic and copies ran while one was open for 14% -> 17% of each run, Pallas kernels for 0% -> 0%
where the time goes in v1:
time: 395 us; the launch traced here: 394 us
  waiting for transfers between devices  264 us (67%)
  local copies, waits for them, and re-layouts  35.3 us (9%)
  matrix products  33.2 us (8%)
  blocking collectives  22.9 us (6%)
  other arithmetic  19.6 us (5%)
  between operations  13.8 us (3%)
  starting transfers between devices  5.09 us (1%)
    reduce_scatter x1, waiting for transfers between devices, body(): lax.psum_scatter(partial_term.astype(jnp.bfloat16), 'tp', scatter_dimensi...  91.8 us
    all_to_all x1, waiting for transfers between devices, body(): lax.all_to_all(jnp.stack([tokens] * lax.axis_size('tp')), 'tp', 0, 0)  73.5 us
    all_gather x1, waiting for transfers between devices, body(): down_local = lax.all_gather(down_cast, 'grp', axis=0, tiled=True)  55.1 us
    all_gather x1, waiting for transfers between devices, body(): lax.all_gather(owned, 'grp', axis=0, tiled=True)  43.9 us
    all_to_all x1, blocking collectives, body(): lax.all_to_all(up_cast, 'tp', split_axis=2, concat_axis=0, tiled=True)  22.9 us
    all_gather x1, local copies, waits for them, and re-layouts, body(): lax.all_gather(owned, 'grp', axis=0, tiled=True)  22.2 us
    dot_general x1, matrix products, body(): jnp.dot(normed, up_local, preferred_element_type=jnp.float32)  17.1 us
    dot_general x1, matrix products, body(): running = jnp.dot(hidden, down_local, preferred_element_type=jnp.float32)  16.1 us
  transfers between devices with their start and end apart: 4, of which 4 were waited for; matrix products, arithmetic and copies ran while one was open for 17% of the time, Pallas kernels for 0%

profile of v1, /device:TPU:1, one launch (start us, length us, event | category | flops | bytes accessed | tf_op | source)
XLA Modules:
  0.0 394.2 jit_solution(8594701417283608860)
XLA Ops:
  7.2 0.0 all-gather.3.cloned.1.call-start
  7.2 6.2 %convert_bitcast_fusion = (bf16[4,8,128,128]{3,1,2,0:T(8,128)(2,1)S(1)}, f32[32,16384]{1,0:T(8,128)}) fusion(f32[32,16384]{1,0:T(8,128)} %param.12, f32[32,16384]{1,0:T(8,128)} %param.15, bf16[32,16384]{1,0:T(8,128)(2,1)} %param.13, f32[32,16384]{1,0:T(8,128)} %param.14), kind=kLoop, calls=%fused_computation.34 | loop fusion | flops 8912896 | bytes 10485760
  13.4 0.2 copy.21
  13.6 0.1 copy.17
  13.8 0.0 copy-start
  13.8 0.0 copy-start.1
  13.8 22.9 %all_to_all.23 = bf16[32,16,8,128]{3,1,0,2:T(8,128)(2,1)} all-to-all(bf16[32,16,8,128]{3,1,0,2:T(8,128)(2,1)S(1)} %copy.17), channel_id=1, replica_groups=mesh['grp'=16,'tp'=8] {'tp'}, dimensions={2} | all-to-all | bytes 2097152 | tf_op jit(solution)/shard_map/all_to_all | solution.py:48
  36.7 0.0 all-gather.3.cloned.1.call-update
  36.7 0.0 all-gather.5.cloned.1.call-start
  36.8 0.0 copy-done
  36.8 0.0 copy-done.1
  36.8 5.5 %fusion.29 = (bf16[128,4096]{1,0:T(8,128)(2,1)}, f32[128,4096]{1,0:T(8,128)}) fusion(f32[128,4096]{1,0:T(8,128)S(1)} %copy-done, f32[128,4096]{1,0:T(8,128)} %param.19, bf16[128,4096]{1,0:T(8,128)(2,1)S(1)} %copy-done.1, f32[128,4096]{1,0:T(8,128)} %param.18), kind=kLoop, calls=%fused_computation.38 | loop fusion | flops 8912896 | bytes 10485760 | tf_op jit(solution)/shard_map/convert_element_type | solution.py:47
  42.3 0.0 all-gather.5.cloned.1.call-update
  42.4 3.9 stack.2
  46.3 0.0 copy-start.2
  46.3 4.8 %all-to-all-start = ((bf16[8,2,320,512]{3,2,1,0:T(8,128)(2,1)}), bf16[8,2,320,512]{3,2,1,0:T(8,128)(2,1)}, u32[]{:S(2)}, u32[]{:S(2)}) async-start(bf16[8,2,320,512]{3,2,1,0:T(8,128)(2,1)} %stack.2), calls=%async_computation | async-start | bytes 10485760 | tf_op jit(solution)/shard_map/all_to_all | solution.py:53
  51.1 0.2 reduce-scatter.2.cloned.1.call-start
  51.3 0.0 copy-done.2
  51.3 73.5 %all-to-all-done = bf16[8,2,320,512]{3,2,1,0:T(8,128)(2,1)} async-done(((bf16[8,2,320,512]{3,2,1,0:T(8,128)(2,1)}), bf16[8,2,320,512]{3,2,1,0:T(8,128)(2,1)}, u32[]{:S(2)}, u32[]{:S(2)}) %all-to-all-start) | async-done | bytes 5242912 | tf_op jit(solution)/shard_map/all_to_all | solution.py:53
  124.8 3.7 fusion
  128.6 4.1 %fusion.3 = bf16[2,320,8,512]{3,1,0,2:T(8,128)(2,1)S(1)} fusion(bf16[8,2,320,512]{3,2,1,0:T(8,128)(2,1)} %all-to-all-done, f32[8,512]{1,0:T(8,128)S(1)} %mul.118, f32[2,320]{1,0:T(2,128)S(1)} %add_rsqrt_fusion), kind=kLoop, calls=%fused_computation.6 | loop fusion | flops 10485760 | bytes 10504704 | tf_op jit(solution)/shard_map/convert_element_type | solution.py:58
  132.7 3.0 copy.16
  135.6 5.8 %copy.20 = bf16[80,8,8,512]{3,1,2,0:T(8,128)(2,1)} copy(bf16[80,8,8,512]{3,2,1,0:T(8,128)(2,1)S(1)} %bitcast.29) | data formatting | bytes 10485760
  141.5 43.9 %all-gather.3.cloned.1.call-done = bf16[4096,16,1,128]{3,1,2,0:T(8,128)(2,1)} async-done(((bf16[256,16,1,128]{3,1,2,0:T(8,128)(2,1)}), bf16[4096,16,1,128]{3,1,2,0:T(8,128)(2,1)}) %all-gather.3.cloned.1.call-update) | async-done | bytes 16777232 | tf_op jit(solution)/shard_map/all_gather | solution.py:49
  185.4 22.2 %copy.19 = bf16[4096,16,1,128]{0,3,1,2:T(8,128)(2,1)} copy(bf16[4096,16,1,128]{3,1,2,0:T(8,128)(2,1)} %all-gather.3.cloned.1.call-done) | data formatting | bytes 33554432 | tf_op jit(solution)/shard_map/all_gather | solution.py:49
  207.6 17.1 %multiply_convert_fusion.1.clone.4 = bf16[640,2048]{1,0:T(8,128)(2,1)S(1)} fusion(bf16[640,4096]{1,0:T(8,128)(2,1)} %bitcast.31, bf16[4096,2048]{0,1:T(8,128)(2,1)} %bitcast.30), kind=kOutput, calls=%fused_computation.7.clone.clone.clone.1 | convolution fusion | flops 10745282560 | bytes 24641536 | tf_op jit(solution)/shard_map/dot_general | solution.py:60
  224.7 55.1 %all-gather.5.cloned.1.call-done = bf16[2048,4096]{1,0:T(8,128)(2,1)} async-done(((bf16[128,4096]{1,0:T(8,128)(2,1)}), bf16[2048,4096]{1,0:T(8,128)(2,1)}) %all-gather.5.cloned.1.call-update) | async-done | bytes 16777232 | tf_op jit(solution)/shard_map/all_gather | solution.py:62
  279.8 16.1 %multiply_convert_fusion = bf16[640,4096]{1,0:T(8,128)(2,1)} fusion(bf16[2048,4096]{1,0:T(8,128)(2,1)} %all-gather.5.cloned.1.call-done, bf16[640,2048]{1,0:T(8,128)(2,1)S(1)} %multiply_convert_fusion.1.clone.4), kind=kOutput, calls=%fused_computation.5 | convolution fusion | flops 10742661120 | bytes 24641536 | tf_op jit(solution)/shard_map/dot_general | solution.py:63
  295.9 0.0 reduce-scatter.2.cloned.1.call-update
  295.9 91.8 %reduce-scatter.2.cloned.1.call-done = bf16[640,512]{1,0:T(8,128)(2,1)} async-done(((bf16[640,4096]{1,0:T(8,128)(2,1)}), bf16[640,512]{1,0:T(8,128)(2,1)}) %reduce-scatter.2.cloned.1.call-update) | async-done | bytes 655376 | tf_op jit(solution)/shard_map/reduce_scatter | solution.py:65
  (2 shorter events, 0.0 us)
Async XLA Ops:
  7.2 178.3 %all-gather.3.cloned.1.call-start = ((), (), s32[]{:S(2)}) async-start(), calls=%async_computation.3 | async-start | bytes 17825792 | tf_op jit(solution)/shard_map/all_gather | solution.py:49
  13.8 23.0 %copy-start = (f32[128,4096]{1,0:T(8,128)S(1)}, f32[128,4096]{1,0:T(8,128)}, u32[]{:S(2)}) copy-start(f32[128,4096]{1,0:T(8,128)} %param.16) | copy-start | bytes 6291460
  13.8 23.0 %copy-start.1 = (bf16[128,4096]{1,0:T(8,128)(2,1)S(1)}, bf16[128,4096]{1,0:T(8,128)(2,1)}, u32[]{:S(2)}) copy-start(bf16[128,4096]{1,0:T(8,128)(2,1)} %param.17) | copy-start | bytes 3145732
  36.7 243.0 %all-gather.5.cloned.1.call-start = ((), (), s32[]{:S(2)}) async-start(), calls=%async_computation.4 | async-start | bytes 17825792 | tf_op jit(solution)/shard_map/all_gather | solution.py:62
  46.3 5.0 %copy-start.2 = (f32[4096]{0:T(1024)S(1)}, f32[4096]{0:T(1024)}, u32[]{:S(2)}) copy-start(f32[4096]{0:T(1024)} %param.11) | copy-start | bytes 49156
  46.3 78.5 %all-to-all-start = ((bf16[8,2,320,512]{3,2,1,0:T(8,128)(2,1)}), bf16[8,2,320,512]{3,2,1,0:T(8,128)(2,1)}, u32[]{:S(2)}, u32[]{:S(2)}) async-start(bf16[8,2,320,512]{3,2,1,0:T(8,128)(2,1)} %stack.2), calls=%async_computation | async-start | bytes 10485760 | tf_op jit(solution)/shard_map/all_to_all | solution.py:53
  51.1 336.6 %reduce-scatter.2.cloned.1.call-start = ((), (), s32[]{:S(2)}) async-start(), calls=%async_computation.5 | async-start | bytes 5898240 | tf_op jit(solution)/shard_map/reduce_scatter | solution.py:65
Sparse Core Ops, SparseCore 0:
  36.9 148.5 all-gather.2
  187.1 92.5 all-gather.4
  296.0 91.6 reduce-scatter.1
